TPU v7x, 32 devices: a whole 2x2x4 slice. The times are simulated.
32 devices in a mesh: seq: 16 (over z, x, core), head: 2 (over y).
Axes of the slice: x: 2, y: 2, z: 4, core: 2. Of those that a mesh axis runs over, the one named last changes fastest.
Arguments:
- query_rows: bfloat16 [4096, 768], P('seq', 'head'), may hold values from -27 to 27
- key_rows: bfloat16 [4096, 768], P('seq', 'head'), may hold values from -6 to 6
- value_rows: bfloat16 [4096, 768], P('seq', 'head'), may hold values from -6 to 6
- rates: float32 [4096, 4], P('seq', 'head'), may hold values from 0.1 to 1
- fw_decay: float32 [16, 4], P('seq', 'head'), may hold values from 0 to 1
- fw_step: float32 [4], P('head'), may hold values from 0.03 to 0.15
- fast_gate: float32 [4, 192, 384], P('head'), may hold values from -0.4375 to 0.4375
- fast_up: float32 [4, 192, 384], P('head'), may hold values from -0.4375 to 0.4375
- fast_down: float32 [4, 384, 192], P('head'), may hold values from -0.3125 to 0.3125
- ttt_gain: float32 [768], P('head'), may hold values from 0.1 to 1.9
- attn_gain: float32 [768], P('head'), may hold values from 0.1 to 1.9
- out_proj: bfloat16 [768, 768], P('head'), may hold values from -0.21875 to 0.21875
Outputs:
- layer_out: bfloat16 [4096, 768], P(('seq', 'head'))
All inputs are finite; a program needn't handle non-finite values.
Results may differ from a plain program's by a relative error of at most 0.0053.
Values may be sent and summed in bfloat16 or wider, within the bound.
A program may use at most 192 MiB of HBM per device.

v0:
```python
import functools
import math

import jax
import jax.numpy as jnp
from jax import lax
from jax.experimental import pallas as pl
from jax.experimental.pallas import tpu as pltpu
from jax.sharding import PartitionSpec as P

WINDOW = 2048
NS_STEPS = 5
GROUP = 4
MESH = pl.DeviceIdType.MESH
BF = jnp.bfloat16
F32 = jnp.float32
coef_a = 3.4445
coef_b = -4.775
coef_c = 2.0315
FAR = -1e30

NN = (((1,), (0,)), ((), ()))
NT = (((1,), (1,)), ((), ()))


def dot1(left, right, dims=NN):
    return lax.dot_general(left, right, dims, preferred_element_type=F32)


def halves(value):
    high = value.astype(BF)
    return high, (value - high.astype(F32)).astype(BF)


def dot3(left, right, dims=NN):
    return dot1(left[0], right[0], dims) + (
        dot1(left[0], right[1], dims) + dot1(left[1], right[0], dims)
    )


def rms_rows(values):
    return values * lax.rsqrt(jnp.mean(values * values, axis=-1, keepdims=True) + 1e-06)


def kernel(
    n_seq,
    n_head,
    q_ref,
    k_ref,
    v_ref,
    rates_ref,
    decay_ref,
    step_ref,
    gate_ref,
    up_ref,
    down_ref,
    tgain_ref,
    again_ref,
    proj_ref,
    out_ref,
    kv,
    dec_own,
    dec_sib,
    upd,
    downt,
    x_out,
    x_in,
    s_out,
    s_in,
    h_out,
    h_in,
    state,
    qpad,
    acc,
    top,
    total,
    mixed,
    p_out,
    p_in,
    kv_send,
    kv_recv,
    dec_sems,
    x_send,
    x_recv,
    s_send,
    s_recv,
    h_send,
    h_recv,
    p_send,
    p_recv,
):
    rows = q_ref.shape[0]
    heads, dim, fast = gate_ref.shape
    part = dim // 2
    scale = 1.0 / math.sqrt(dim)
    reach = WINDOW // rows
    n_group = n_seq // GROUP
    n_chip = n_seq // 2
    me = lax.axis_index("seq")
    head = lax.axis_index("head")
    group = me // GROUP
    member = me % GROUP
    side = member // 2
    core = member % 2
    chip = me // 2
    sibling = me + 1 - 2 * core
    across = me + 2 - 4 * side
    onward = me + GROUP
    next_chip = me + 2

    barrier = pltpu.get_barrier_semaphore()

    def greet(seq_pos, head_pos):
        pl.semaphore_signal(barrier, inc=1, device_id=(seq_pos, head_pos), device_id_type=MESH)

    greet(sibling, head)
    greet(across, head)
    expected = jnp.int32(2 + n_head - 1)
    for step in (GROUP, -GROUP, 2, -2):
        there = (me + step >= 0) & (me + step < n_seq)
        pl.when(there)(functools.partial(greet, me + step, head))
        expected = expected + there.astype(jnp.int32)
    for hop in range(1, n_head):
        greet(me, lax.rem(head + hop, n_head))

    own = reach + member
    kv[own, 0] = k_ref[...]
    kv[own, 1] = v_ref[...]
    dec_own[...] = jnp.zeros(dec_own.shape, F32)
    for h in range(heads):
        dec_own[h : h + 1, :] = jnp.broadcast_to(decay_ref[0:1, h : h + 1], (1, 128))
    pl.semaphore_wait(barrier, expected)

    def kv_copy(from_slot, to_slot, number, seq_pos):
        return pltpu.make_async_remote_copy(
            src_ref=kv.at[from_slot],
            dst_ref=kv.at[to_slot],
            send_sem=kv_send.at[number],
            recv_sem=kv_recv.at[to_slot],
            device_id=(seq_pos, head),
            device_id_type=MESH,
        )

    def slot_of(distance):
        return reach + member - distance

    has_next = group + 1 < n_group
    sends = [
        (has_next, own, own - GROUP, 0, onward),
        (side == 0, own, own, 1, across),
        (core == 0, own, own, 2, sibling),
        (has_next & (me >= 4), slot_of(4), slot_of(8), 3, onward),
        (me >= 4, slot_of(4), slot_of(4), 4, across),
        (me >= 4, slot_of(4), slot_of(4), 5, sibling),
        ((me >= 8) & (side == 1), slot_of(8), slot_of(8), 6, across),
        ((me >= 8) & (core == 1), slot_of(8), slot_of(8), 7, sibling),
        (me >= 2, slot_of(2), slot_of(2), 8, sibling),
        (me >= 6, slot_of(6), slot_of(6), 9, sibling),
    ]

    def start_send(number):
        cond, from_slot, to_slot, _, target = sends[number]

        @pl.when(cond)
        def _():
            kv_copy(jnp.maximum(from_slot, 0), jnp.maximum(to_slot, 0), number, target).start()

    def await_block(distance):
        slot = slot_of(distance)
        pltpu.make_async_copy(kv.at[slot], kv.at[slot], kv_recv.at[slot]).wait()

    def arrive(distance, numbers):
        @pl.when(me >= distance)
        def _():
            await_block(distance)
            for number in numbers:
                start_send(number)

    dec_copy = pltpu.make_async_remote_copy(
        src_ref=dec_own,
        dst_ref=dec_sib,
        send_sem=dec_sems.at[0],
        recv_sem=dec_sems.at[1],
        device_id=(sibling, head),
        device_id_type=MESH,
    )
    dec_copy.start()
    for number in (0, 1, 2):
        start_send(number)

    for h in range(heads):
        cols = slice(h * dim, (h + 1) * dim)
        key_norm = rms_rows(k_ref[...].astype(F32)[:, cols])
        err = -rates_ref[:, h : h + 1] * v_ref[...].astype(F32)[:, cols]
        downt[h] = down_ref[h].T
        key_pair = halves(key_norm)
        pre_gate = dot3(key_pair, halves(gate_ref[h]))
        pre_up = dot3(key_pair, halves(up_ref[h]))
        sig = jax.nn.sigmoid(pre_gate)
        active = pre_gate * sig
        back = dot3(halves(err), halves(downt[h]))
        key_t = halves(key_norm.T)
        grads = (
            dot3(key_t, halves(back * pre_up * (sig * (1.0 + pre_gate * (1.0 - sig))))),
            dot3(key_t, halves(back * active)),
            dot3(halves(err.T), halves(active * pre_up)),
        )
        for i, grad in enumerate(grads):
            size = jnp.sum(jnp.sum(grad * grad, axis=1, keepdims=True), axis=0, keepdims=True)
            upd[3 * h + i] = grad / (jnp.sqrt(size) + 1e-07)

    def sweep(turn, carry):
        for j in range(3 * heads):
            current = upd[j]
            low = current.astype(BF)
            gram = dot1(low, low, NT)
            gram_low = gram.astype(BF)
            poly = coef_b * gram + coef_c * dot1(gram_low, gram_low)
            upd[j] = coef_a * current + dot1(poly.astype(BF), low)

        @pl.when(turn == 1)
        def _():
            arrive(4, (3, 4, 5))

        @pl.when(turn == 3)
        def _():
            arrive(2, (8,))

        return carry

    lax.fori_loop(0, NS_STEPS, sweep, 0)

    mine_at = pl.multiple_of(core * part, part)
    other_at = pl.multiple_of((1 - core) * part, part)

    def pair_copy(source, target, send, recv, j, seq_pos):
        return pltpu.make_async_remote_copy(
            src_ref=source.at[j],
            dst_ref=target.at[j],
            send_sem=send.at[j],
            recv_sem=recv.at[j],
            device_id=(seq_pos, head),
            device_id_type=MESH,
        )

    x_copy = lambda j: pair_copy(x_out, x_in, x_send, x_recv, j, sibling)
    s_copy = lambda j: pair_copy(s_out, s_in, s_send, s_recv, j, next_chip)
    h_copy = lambda j: pair_copy(h_out, h_in, h_send, h_recv, j, sibling)

    for j in range(3 * heads):
        h = j // 3
        upd[j] = -step_ref[0:1, h : h + 1] * upd[j]
        x_out[j] = upd[j, pl.ds(other_at, part), :].astype(BF)
        x_copy(j).start()
    dec_copy.wait()

    @pl.when(chip == 0)
    def _():
        s_in[...] = jnp.zeros(s_in.shape, BF)

    arrive(8, (6, 7))
    arrive(6, (9,))

    first = core == 0

    def chain():
        def link(j, carry):
            h = j // 3
            x_copy(j).wait_recv()

            @pl.when(chip > 0)
            def _():
                s_copy(j).wait_recv()

            d_own = dec_own[pl.ds(h, 1), :][:, 0:1]
            d_sib = dec_sib[pl.ds(h, 1), :][:, 0:1]
            decay0 = jnp.where(first, d_own, d_sib)
            decay1 = jnp.where(first, d_sib, d_own)
            u_own = upd[j, pl.ds(mine_at, part), :]
            u_sib = x_in[j].astype(F32)
            u0 = jnp.where(first, u_own, u_sib)
            u1 = jnp.where(first, u_sib, u_own)
            before = s_in[j].astype(F32)
            middle = decay0 * before + u0

            @pl.when(chip + 1 < n_chip)
            def _():
                s_out[j] = (decay1 * middle + u1).astype(BF)
                s_copy(j).start()

            h_out[j] = jnp.where(first, middle, before).astype(BF)
            h_copy(j).start()
            state[j, pl.ds(mine_at, part), :] = jnp.where(first, before, middle)
            return carry

        lax.fori_loop(0, 3 * heads, link, 0)

    lane = lax.broadcasted_iota(jnp.int32, (rows, 256), 1)
    starts = [0, heads * dim - 256]
    for h in range(heads):
        begin = h * dim - starts[h]
        inside = (lane >= begin) & (lane < begin + dim)
        wide = q_ref[:, starts[h] : starts[h] + 256].astype(F32)
        qpad[h] = jnp.where(inside, wide, 0.0).astype(BF)
    acc[...] = jnp.zeros(acc.shape, F32)
    top[...] = jnp.full(top.shape, FAR, F32)
    total[...] = jnp.zeros(total.shape, F32)
    gap = lax.broadcasted_iota(jnp.int32, (rows, rows), 0) - lax.broadcasted_iota(
        jnp.int32, (rows, rows), 1
    )

    def attend(distance, carry):
        @pl.when(2 * chip == distance)
        def _():
            chain()

        @pl.when(me >= distance)
        def _():
            @pl.when(distance % 2 == 1)
            def _():
                await_block(distance)

            slot = slot_of(distance)
            back = gap + distance * rows
            allowed = (back >= 0) & (back < WINDOW)
            for h in range(heads):
                cols = slice(starts[h], starts[h] + 256)
                scores = dot1(qpad[h], kv[slot, 0, :, cols], NT) * scale
                scores = jnp.where(allowed, scores, FAR)
                old_top = top[h][:, 0:1]
                new_top = jnp.maximum(old_top, jnp.max(scores, axis=1, keepdims=True))
                weights = jnp.exp(scores - new_top)
                shrink = jnp.exp(old_top - new_top)
                total[h] = jnp.broadcast_to(
                    total[h][:, 0:1] * shrink + jnp.sum(weights, axis=1, keepdims=True), (rows, 128)
                )
                acc[h] = acc[h] * shrink + dot1(weights.astype(BF), kv[slot, 1, :, cols])
                top[h] = jnp.broadcast_to(new_top, (rows, 128))

        return carry

    lax.fori_loop(0, reach + 1, attend, 0)

    @pl.when(2 * chip > reach)
    def _():
        chain()

    for j in range(3 * heads):
        h_copy(j).wait_recv()
        state[j, pl.ds(other_at, part), :] = h_in[j].astype(F32)

    for h in range(heads):
        cols = slice(h * dim, (h + 1) * dim)
        query = halves(rms_rows(q_ref[...].astype(F32)[:, cols]))
        pre_gate = dot3(query, halves(gate_ref[h] + state[3 * h]))
        pre_up = dot3(query, halves(up_ref[h] + state[3 * h + 1]))
        hidden = pre_gate * jax.nn.sigmoid(pre_gate) * pre_up
        applied = dot3(halves(hidden), halves(downt[h] + state[3 * h + 2]), NT)
        begin = h * dim - starts[h]
        attended = acc[h][:, begin : begin + dim] / total[h][:, 0:1]
        mixed[h] = (
            rms_rows(applied) * tgain_ref[...][:, cols]
            + rms_rows(attended) * again_ref[...][:, cols]
        ).astype(BF)

    share = rows // n_head

    def project(target):
        at = pl.multiple_of(target * share, share)
        result = dot1(mixed[0, pl.ds(at, share), :], proj_ref[0:dim, :])
        for h in range(1, heads):
            result = result + dot1(
                mixed[h, pl.ds(at, share), :], proj_ref[h * dim : (h + 1) * dim, :]
            )
        return result

    def p_copy(hop):
        return pltpu.make_async_remote_copy(
            src_ref=p_out.at[hop - 1],
            dst_ref=p_in.at[hop - 1],
            send_sem=p_send.at[hop - 1],
            recv_sem=p_recv.at[hop - 1],
            device_id=(me, lax.rem(head + hop, n_head)),
            device_id_type=MESH,
        )

    for hop in range(1, n_head):
        p_out[hop - 1] = project(lax.rem(head + hop, n_head)).astype(BF)
        p_copy(hop).start()
    result = project(head)
    for hop in range(1, n_head):
        p_copy(hop).wait_recv()
        result = result + p_in[hop - 1].astype(F32)
    out_ref[...] = result.astype(BF)

    for number, (cond, from_slot, to_slot, _, target) in enumerate(sends):

        @pl.when(cond)
        def _():
            kv_copy(
                jnp.maximum(from_slot, 0), jnp.maximum(to_slot, 0), number, target
            ).wait_send()

    for j in range(3 * heads):
        x_copy(j).wait_send()
        h_copy(j).wait_send()

        @pl.when(chip + 1 < n_chip)
        def _():
            s_copy(j).wait_send()

    for hop in range(1, n_head):
        p_copy(hop).wait_send()


def local(
    n_seq,
    n_head,
    query_rows,
    key_rows,
    value_rows,
    rates,
    fw_decay,
    fw_step,
    fast_gate,
    fast_up,
    fast_down,
    ttt_gain,
    attn_gain,
    out_proj,
):
    rows, cols = query_rows.shape
    heads, dim, fast = fast_gate.shape
    width = out_proj.shape[1]
    share = rows // n_head
    mats = 3 * heads
    part = dim // 2
    slots = WINDOW // rows + GROUP
    dma = pltpu.SemaphoreType.DMA
    piece = pltpu.VMEM((mats, part, fast), BF)
    return pl.pallas_call(
        functools.partial(kernel, n_seq, n_head),
        out_shape=jax.ShapeDtypeStruct((share, width), BF),
        in_specs=[pl.BlockSpec(memory_space=pltpu.VMEM)] * 12,
        out_specs=pl.BlockSpec(memory_space=pltpu.VMEM),
        scratch_shapes=[
            pltpu.VMEM((slots, 2, rows, cols), BF),
            pltpu.VMEM((8, 128), F32),
            pltpu.VMEM((8, 128), F32),
            pltpu.VMEM((mats, dim, fast), F32),
            pltpu.VMEM((heads, dim, fast), F32),
            piece,
            piece,
            piece,
            piece,
            piece,
            piece,
            pltpu.VMEM((mats, dim, fast), F32),
            pltpu.VMEM((heads, rows, 256), BF),
            pltpu.VMEM((heads, rows, 256), F32),
            pltpu.VMEM((heads, rows, 128), F32),
            pltpu.VMEM((heads, rows, 128), F32),
            pltpu.VMEM((heads, rows, dim), BF),
            pltpu.VMEM((n_head - 1, share, width), BF),
            pltpu.VMEM((n_head - 1, share, width), BF),
            dma((10,)),
            dma((slots,)),
            dma((2,)),
            dma((mats,)),
            dma((mats,)),
            dma((mats,)),
            dma((mats,)),
            dma((mats,)),
            dma((mats,)),
            dma((n_head - 1,)),
            dma((n_head - 1,)),
        ],
        compiler_params=pltpu.CompilerParams(
            collective_id=0, has_side_effects=True, vmem_limit_bytes=48 * 1024 * 1024
        ),
    )(
        query_rows,
        key_rows,
        value_rows,
        rates,
        fw_decay,
        fw_step.reshape(1, -1),
        fast_gate,
        fast_up,
        fast_down,
        ttt_gain.reshape(1, -1),
        attn_gain.reshape(1, -1),
        out_proj,
    )


def solution(mesh):
    in_specs = (
        P("seq", "head"),
        P("seq", "head"),
        P("seq", "head"),
        P("seq", "head"),
        P("seq", "head"),
        P("head"),
        P("head", None, None),
        P("head", None, None),
        P("head", None, None),
        P("head"),
        P("head"),
        P("head", None),
    )
    out_specs = P(("seq", "head"), None)
    body = functools.partial(local, mesh.shape["seq"], mesh.shape["head"])
    return jax.shard_map(body, mesh=mesh, in_specs=in_specs, out_specs=out_specs, check_vma=False)
```

profile of v0, /device:TPU:27, one launch (start us, length us, event | category | flops | bytes accessed | tf_op | source)
XLA Modules:
  0.0 70.0 jit_solution(3063957844197912328)
XLA Ops:
  0.0 0.0 copy-start.9
  0.0 0.7 reshape.10.tgain_ref
  0.7 0.0 copy-done.9
  0.7 0.0 copy-start.8
  0.7 0.7 copy-done.8
  1.4 0.0 copy-start.6
  1.4 0.0 copy-start.7
  1.4 0.1 copy.13.rates_ref
  1.5 0.0 copy-start
  1.5 0.0 copy-start.1
  1.6 0.0 copy-start.3
  1.6 1.4 %copy.14.down_ref = f32[2,384,192]{2,1,0:T(8,128)S(1)} copy(f32[2,384,192]{1,2,0:T(8,128)} %param.20) | data formatting | bytes 1179648 | tf_op args[8]
  3.0 0.0 copy-done.6
  3.0 0.0 copy-done.7
  3.0 0.0 copy-done
  3.0 0.0 copy-done.1
  3.0 0.0 copy-done.3
  3.1 0.0 copy-start.2
  3.1 1.1 %copy-done.2 = bf16[384,768]{1,0:T(8,128)(2,1)S(1)} copy-done((bf16[384,768]{1,0:T(8,128)(2,1)S(1)}, bf16[384,768]{1,0:T(8,128)(2,1)}, u32[]{:S(2)}) %copy-start.2) | copy-done | bytes 589848
  4.1 0.0 copy-start.4
  4.1 0.9 %copy-done.4 = bf16[256,384]{1,0:T(8,128)(2,1)S(1)} copy-done((bf16[256,384]{1,0:T(8,128)(2,1)S(1)}, bf16[256,384]{1,0:T(8,128)(2,1)}, u32[]{:S(2)}) %copy-start.4) | copy-done | bytes 196632
  5.1 0.9 %copy-done.5 = bf16[256,384]{1,0:T(8,128)(2,1)S(1)} copy-done((bf16[256,384]{1,0:T(8,128)(2,1)S(1)}, bf16[256,384]{1,0:T(8,128)(2,1)}, u32[]{:S(2)}) %copy-start.5) | copy-done | bytes 196632
  6.0 63.4 %shard_map.118 = bf16[128,768]{1,0:T(8,128)(2,1)S(1)} custom-call(bf16[256,384]{1,0:T(8,128)(2,1)S(1)} %copy-done.3, bf16[256,384]{1,0:T(8,128)(2,1)S(1)} %copy-done.4, bf16[256,384]{1,0:T(8,128)(2,1)S(1)} %copy-done.5, f32[256,2]{1,0:T(8,128)S(1)} %copy.13.rates_ref, f32[1,2]{1,0:T(1,128)S(1)} %copy-done.6, f32[1,2]{1,0:T(1,128)S(1)} %bitcast.1, ...), custom_call_target="tpu_custom_call" | custom-call | tf_op jit(solution)/shard_map/pallas_call | solution.py:441
  69.4 0.7 copy.16
  (2 shorter events, 0.0 us)
Async XLA Ops:
  0.0 0.7 %copy-start.9 = (f32[384]{0:T(512)S(1)}, f32[384]{0:T(512)}, u32[]{:S(2)}) copy-start(f32[384]{0:T(512)} %param.22) | copy-start | bytes 4612
  0.7 0.7 copy-start.8
  1.4 1.6 %copy-start.6 = (f32[1,2]{1,0:T(1,128)S(1)}, f32[1,2]{1,0:T(1,128)}, u32[]{:S(2)}) copy-start(f32[1,2]{1,0:T(1,128)} %decay_ref.1) | copy-start | bytes 28
  1.4 1.6 %copy-start.7 = (f32[2]{0:T(128)S(1)}, f32[2]{0:T(128)}, u32[]{:S(2)}) copy-start(f32[2]{0:T(128)} %param.17) | copy-start | bytes 28
  1.5 1.5 %copy-start = (f32[2,192,384]{2,1,0:T(8,128)S(1)}, f32[2,192,384]{2,1,0:T(8,128)}, u32[]{:S(2)}) copy-start(f32[2,192,384]{2,1,0:T(8,128)} %gate_ref.1) | copy-start | bytes 1769476
  1.5 1.5 %copy-start.1 = (f32[2,192,384]{2,1,0:T(8,128)S(1)}, f32[2,192,384]{2,1,0:T(8,128)}, u32[]{:S(2)}) copy-start(f32[2,192,384]{2,1,0:T(8,128)} %up_ref.1) | copy-start | bytes 1769476
  1.6 1.5 %copy-start.3 = (bf16[256,384]{1,0:T(8,128)(2,1)S(1)}, bf16[256,384]{1,0:T(8,128)(2,1)}, u32[]{:S(2)}) copy-start(bf16[256,384]{1,0:T(8,128)(2,1)} %q_ref.1) | copy-start | bytes 589828
  3.1 1.1 %copy-start.2 = (bf16[384,768]{1,0:T(8,128)(2,1)S(1)}, bf16[384,768]{1,0:T(8,128)(2,1)}, u32[]{:S(2)}) copy-start(bf16[384,768]{1,0:T(8,128)(2,1)} %proj_ref.1) | copy-start | bytes 1769476
  4.1 0.9 %copy-start.4 = (bf16[256,384]{1,0:T(8,128)(2,1)S(1)}, bf16[256,384]{1,0:T(8,128)(2,1)}, u32[]{:S(2)}) copy-start(bf16[256,384]{1,0:T(8,128)(2,1)} %k_ref.1) | copy-start | bytes 589828
  5.0 0.9 %copy-start.5 = (bf16[256,384]{1,0:T(8,128)(2,1)S(1)}, bf16[256,384]{1,0:T(8,128)(2,1)}, u32[]{:S(2)}) copy-start(bf16[256,384]{1,0:T(8,128)(2,1)} %v_ref.1) | copy-start | bytes 589828
where the time goes:
time: 70.3 us; the launch traced here: 70 us
  Pallas kernels  63.4 us (90%)
  local copies, waits for them, and re-layouts  6.56 us (9%)
    pallas_call x1, Pallas kernels, local(): pl.pallas_call(functools.partial(kernel, n_seq, n_head), out_shape=jax.Sh...  63.4 us
    unnamed x23, local copies, waits for them, and re-layouts  5.86 us

commit v1 on v0

--- a/solution.py
+++ b/solution.py
@@ -11,6 +11,7 @@
 WINDOW = 2048
 NS_STEPS = 5
 GROUP = 4
+SPLIT = 2
 MESH = pl.DeviceIdType.MESH
 BF = jnp.bfloat16
 F32 = jnp.float32
@@ -45,26 +46,35 @@
 def kernel(
     n_seq,
     n_head,
-    q_ref,
-    k_ref,
-    v_ref,
+    q_hbm,
+    k_hbm,
+    v_hbm,
     rates_ref,
     decay_ref,
     step_ref,
+    gate_hbm,
+    up_hbm,
+    downt_hbm,
+    tgain_ref,
+    again_ref,
+    proj_hbm,
+    out_ref,
+    q_ref,
     gate_ref,
     up_ref,
-    down_ref,
-    tgain_ref,
-    again_ref,
+    downt,
     proj_ref,
-    out_ref,
     kv,
     dec_own,
     dec_sib,
+    dec_chip,
+    dec_across,
     upd,
-    downt,
     x_out,
     x_in,
+    t_own,
+    t_out,
+    t_in,
     s_out,
     s_in,
     h_out,
@@ -77,11 +87,14 @@
     mixed,
     p_out,
     p_in,
+    load_sems,
     kv_send,
     kv_recv,
     dec_sems,
     x_send,
     x_recv,
+    t_send,
+    t_recv,
     s_send,
     s_recv,
     h_send,
@@ -90,23 +103,40 @@
     p_recv,
 ):
     rows = q_ref.shape[0]
-    heads, dim, fast = gate_ref.shape
+    heads, dim, _ = gate_ref.shape
     part = dim // 2
+    chunk = part // SPLIT
+    pieces = 3 * heads * SPLIT
     scale = 1.0 / math.sqrt(dim)
     reach = WINDOW // rows
     n_group = n_seq // GROUP
-    n_chip = n_seq // 2
     me = lax.axis_index("seq")
     head = lax.axis_index("head")
     group = me // GROUP
     member = me % GROUP
     side = member // 2
     core = member % 2
-    chip = me // 2
     sibling = me + 1 - 2 * core
     across = me + 2 - 4 * side
     onward = me + GROUP
-    next_chip = me + 2
+    own = reach + member
+
+    loads = [
+        pltpu.make_async_copy(source, target, load_sems.at[i])
+        for i, (source, target) in enumerate(
+            (
+                (k_hbm, kv.at[own, 0]),
+                (v_hbm, kv.at[own, 1]),
+                (gate_hbm, gate_ref),
+                (up_hbm, up_ref),
+                (downt_hbm, downt),
+                (q_hbm, q_ref),
+                (proj_hbm, proj_ref),
+            )
+        )
+    ]
+    for load in loads:
+        load.start()
 
     barrier = pltpu.get_barrier_semaphore()
 
@@ -116,19 +146,18 @@
     greet(sibling, head)
     greet(across, head)
     expected = jnp.int32(2 + n_head - 1)
-    for step in (GROUP, -GROUP, 2, -2):
+    for step in (GROUP, -GROUP):
         there = (me + step >= 0) & (me + step < n_seq)
         pl.when(there)(functools.partial(greet, me + step, head))
         expected = expected + there.astype(jnp.int32)
     for hop in range(1, n_head):
         greet(me, lax.rem(head + hop, n_head))
 
-    own = reach + member
-    kv[own, 0] = k_ref[...]
-    kv[own, 1] = v_ref[...]
     dec_own[...] = jnp.zeros(dec_own.shape, F32)
     for h in range(heads):
         dec_own[h : h + 1, :] = jnp.broadcast_to(decay_ref[0:1, h : h + 1], (1, 128))
+    loads[0].wait()
+    loads[1].wait()
     pl.semaphore_wait(barrier, expected)
 
     def kv_copy(from_slot, to_slot, number, seq_pos):
@@ -188,11 +217,14 @@
     for number in (0, 1, 2):
         start_send(number)
 
+    for load in loads[2:5]:
+        load.wait()
+
     for h in range(heads):
         cols = slice(h * dim, (h + 1) * dim)
-        key_norm = rms_rows(k_ref[...].astype(F32)[:, cols])
-        err = -rates_ref[:, h : h + 1] * v_ref[...].astype(F32)[:, cols]
-        downt[h] = down_ref[h].T
+        key_norm = rms_rows(kv[own, 0].astype(F32)[:, cols])
+        rate = jnp.broadcast_to(rates_ref[h : h + 1, :], (8, rows)).T[:, 0:1]
+        err = -rate * kv[own, 1].astype(F32)[:, cols]
         key_pair = halves(key_norm)
         pre_gate = dot3(key_pair, halves(gate_ref[h]))
         pre_up = dot3(key_pair, halves(up_ref[h]))
@@ -243,58 +275,105 @@
             device_id_type=MESH,
         )
 
-    x_copy = lambda j: pair_copy(x_out, x_in, x_send, x_recv, j, sibling)
-    s_copy = lambda j: pair_copy(s_out, s_in, s_send, s_recv, j, next_chip)
-    h_copy = lambda j: pair_copy(h_out, h_in, h_send, h_recv, j, sibling)
-
-    for j in range(3 * heads):
-        h = j // 3
-        upd[j] = -step_ref[0:1, h : h + 1] * upd[j]
-        x_out[j] = upd[j, pl.ds(other_at, part), :].astype(BF)
-        x_copy(j).start()
+    x_copy = lambda p: pair_copy(x_out, x_in, x_send, x_recv, p, sibling)
+    t_copy = lambda p: pair_copy(t_out, t_in, t_send, t_recv, p, across)
+    s_copy = lambda p: pair_copy(s_out, s_in, s_send, s_recv, p, onward)
+    h_copy = lambda p: pair_copy(h_out, h_in, h_send, h_recv, p, sibling)
+
+    def rows_at(p, base):
+        return pl.ds(pl.multiple_of(base + (p % SPLIT) * chunk, chunk), chunk)
+
+    for p in range(pieces):
+        j = p // SPLIT
+        if p % SPLIT == 0:
+            upd[j] = -step_ref[0:1, j // 3 : j // 3 + 1] * upd[j]
+        x_out[p] = upd[j, rows_at(p, other_at), :].astype(BF)
+        x_copy(p).start()
     dec_copy.wait()
-
-    @pl.when(chip == 0)
+    dec_chip[...] = dec_own[...] * dec_sib[...]
+    dec_chip_copy = pltpu.make_async_remote_copy(
+        src_ref=dec_chip,
+        dst_ref=dec_across,
+        send_sem=dec_sems.at[2],
+        recv_sem=dec_sems.at[3],
+        device_id=(across, head),
+        device_id_type=MESH,
+    )
+    dec_chip_copy.start()
+
+    @pl.when(group == 0)
     def _():
         s_in[...] = jnp.zeros(s_in.shape, BF)
 
+    first = core == 0
+
+    def of_pair(p):
+        j = p // SPLIT
+        h = j // 3
+        d_own = dec_own[pl.ds(h, 1), :][:, 0:1]
+        d_sib = dec_sib[pl.ds(h, 1), :][:, 0:1]
+        u_own = upd[j, rows_at(p, mine_at), :]
+        u_sib = x_in[p].astype(F32)
+        return (
+            jnp.where(first, d_own, d_sib),
+            jnp.where(first, d_sib, d_own),
+            jnp.where(first, u_own, u_sib),
+            jnp.where(first, u_sib, u_own),
+        )
+
+    def sum_pair(p, carry):
+        x_copy(p).wait_recv()
+        _, decay1, u0, u1 = of_pair(p)
+        both = decay1 * u0 + u1
+        t_own[p] = both
+        t_out[p] = both.astype(BF)
+        t_copy(p).start()
+        return carry
+
+    lax.fori_loop(0, pieces, sum_pair, 0)
+    dec_chip_copy.wait()
+
     arrive(8, (6, 7))
     arrive(6, (9,))
 
-    first = core == 0
+    near = side == 0
 
     def chain():
-        def link(j, carry):
-            h = j // 3
-            x_copy(j).wait_recv()
-
-            @pl.when(chip > 0)
+        def link(p, carry):
+            h = p // SPLIT // 3
+            t_copy(p).wait_recv()
+
+            @pl.when(group > 0)
             def _():
-                s_copy(j).wait_recv()
-
-            d_own = dec_own[pl.ds(h, 1), :][:, 0:1]
-            d_sib = dec_sib[pl.ds(h, 1), :][:, 0:1]
-            decay0 = jnp.where(first, d_own, d_sib)
-            decay1 = jnp.where(first, d_sib, d_own)
-            u_own = upd[j, pl.ds(mine_at, part), :]
-            u_sib = x_in[j].astype(F32)
-            u0 = jnp.where(first, u_own, u_sib)
-            u1 = jnp.where(first, u_sib, u_own)
-            before = s_in[j].astype(F32)
+                s_copy(p).wait_recv()
+
+            c_own = dec_chip[pl.ds(h, 1), :][:, 0:1]
+            c_far = dec_across[pl.ds(h, 1), :][:, 0:1]
+            chip0 = jnp.where(near, c_own, c_far)
+            chip1 = jnp.where(near, c_far, c_own)
+            t_far = t_in[p].astype(F32)
+            t_mine = t_own[p]
+            t0 = jnp.where(near, t_mine, t_far)
+            t1 = jnp.where(near, t_far, t_mine)
+            enter = s_in[p].astype(F32)
+            halfway = chip0 * enter + t0
+
+            @pl.when(has_next)
+            def _():
+                s_out[p] = (chip1 * halfway + t1).astype(BF)
+                s_copy(p).start()
+
+            decay0, _, u0, _ = of_pair(p)
+            before = jnp.where(near, enter, halfway)
             middle = decay0 * before + u0
-
-            @pl.when(chip + 1 < n_chip)
-            def _():
-                s_out[j] = (decay1 * middle + u1).astype(BF)
-                s_copy(j).start()
-
-            h_out[j] = jnp.where(first, middle, before).astype(BF)
-            h_copy(j).start()
-            state[j, pl.ds(mine_at, part), :] = jnp.where(first, before, middle)
+            h_out[p] = jnp.where(first, middle, before).astype(BF)
+            h_copy(p).start()
+            state[p // SPLIT, rows_at(p, mine_at), :] = jnp.where(first, before, middle)
             return carry
 
-        lax.fori_loop(0, 3 * heads, link, 0)
-
+        lax.fori_loop(0, pieces, link, 0)
+
+    loads[5].wait()
     lane = lax.broadcasted_iota(jnp.int32, (rows, 256), 1)
     starts = [0, heads * dim - 256]
     for h in range(heads):
@@ -310,7 +389,7 @@
     )
 
     def attend(distance, carry):
-        @pl.when(2 * chip == distance)
+        @pl.when(3 * group == distance)
         def _():
             chain()
 
@@ -341,13 +420,14 @@
 
     lax.fori_loop(0, reach + 1, attend, 0)
 
-    @pl.when(2 * chip > reach)
+    @pl.when(3 * group > reach)
     def _():
         chain()
 
-    for j in range(3 * heads):
-        h_copy(j).wait_recv()
-        state[j, pl.ds(other_at, part), :] = h_in[j].astype(F32)
+    loads[6].wait()
+    for p in range(pieces):
+        h_copy(p).wait_recv()
+        state[p // SPLIT, rows_at(p, other_at), :] = h_in[p].astype(F32)
 
     for h in range(heads):
         cols = slice(h * dim, (h + 1) * dim)
@@ -359,8 +439,8 @@
         begin = h * dim - starts[h]
         attended = acc[h][:, begin : begin + dim] / total[h][:, 0:1]
         mixed[h] = (
-            rms_rows(applied) * tgain_ref[...][:, cols]
-            + rms_rows(attended) * again_ref[...][:, cols]
+            rms_rows(applied) * tgain_ref[...].reshape(1, -1)[:, cols]
+            + rms_rows(attended) * again_ref[...].reshape(1, -1)[:, cols]
         ).astype(BF)
 
     share = rows // n_head
@@ -401,13 +481,14 @@
                 jnp.maximum(from_slot, 0), jnp.maximum(to_slot, 0), number, target
             ).wait_send()
 
-    for j in range(3 * heads):
-        x_copy(j).wait_send()
-        h_copy(j).wait_send()
-
-        @pl.when(chip + 1 < n_chip)
-        def _():
-            s_copy(j).wait_send()
+    for p in range(pieces):
+        x_copy(p).wait_send()
+        t_copy(p).wait_send()
+        h_copy(p).wait_send()
+
+        @pl.when(has_next)
+        def _():
+            s_copy(p).wait_send()
 
     for hop in range(1, n_head):
         p_copy(hop).wait_send()
@@ -434,21 +515,33 @@
     width = out_proj.shape[1]
     share = rows // n_head
     mats = 3 * heads
-    part = dim // 2
     slots = WINDOW // rows + GROUP
     dma = pltpu.SemaphoreType.DMA
-    piece = pltpu.VMEM((mats, part, fast), BF)
+    pieces = mats * SPLIT
+    chunk = dim // 2 // SPLIT
+    piece = pltpu.VMEM((pieces, chunk, fast), BF)
+    moved = pl.BlockSpec(memory_space=pl.ANY)
+    small = pl.BlockSpec(memory_space=pltpu.VMEM)
     return pl.pallas_call(
         functools.partial(kernel, n_seq, n_head),
         out_shape=jax.ShapeDtypeStruct((share, width), BF),
-        in_specs=[pl.BlockSpec(memory_space=pltpu.VMEM)] * 12,
+        in_specs=[moved] * 3 + [small] * 3 + [moved] * 3 + [small] * 2 + [moved],
         out_specs=pl.BlockSpec(memory_space=pltpu.VMEM),
         scratch_shapes=[
+            pltpu.VMEM((rows, cols), BF),
+            pltpu.VMEM((heads, dim, fast), F32),
+            pltpu.VMEM((heads, dim, fast), F32),
+            pltpu.VMEM((heads, dim, fast), F32),
+            pltpu.VMEM((cols, width), BF),
             pltpu.VMEM((slots, 2, rows, cols), BF),
             pltpu.VMEM((8, 128), F32),
             pltpu.VMEM((8, 128), F32),
+            pltpu.VMEM((8, 128), F32),
+            pltpu.VMEM((8, 128), F32),
             pltpu.VMEM((mats, dim, fast), F32),
-            pltpu.VMEM((heads, dim, fast), F32),
+            piece,
+            piece,
+            pltpu.VMEM((pieces, chunk, fast), F32),
             piece,
             piece,
             piece,
@@ -463,33 +556,36 @@
             pltpu.VMEM((heads, rows, dim), BF),
             pltpu.VMEM((n_head - 1, share, width), BF),
             pltpu.VMEM((n_head - 1, share, width), BF),
+            dma((7,)),
             dma((10,)),
             dma((slots,)),
-            dma((2,)),
-            dma((mats,)),
-            dma((mats,)),
-            dma((mats,)),
-            dma((mats,)),
-            dma((mats,)),
-            dma((mats,)),
+            dma((4,)),
+            dma((pieces,)),
+            dma((pieces,)),
+            dma((pieces,)),
+            dma((pieces,)),
+            dma((pieces,)),
+            dma((pieces,)),
+            dma((pieces,)),
+            dma((pieces,)),
             dma((n_head - 1,)),
             dma((n_head - 1,)),
         ],
         compiler_params=pltpu.CompilerParams(
-            collective_id=0, has_side_effects=True, vmem_limit_bytes=48 * 1024 * 1024
+            collective_id=0, has_side_effects=True, vmem_limit_bytes=56 * 1024 * 1024
         ),
     )(
         query_rows,
         key_rows,
         value_rows,
-        rates,
+        rates.T,
         fw_decay,
         fw_step.reshape(1, -1),
         fast_gate,
         fast_up,
-        fast_down,
-        ttt_gain.reshape(1, -1),
-        attn_gain.reshape(1, -1),
+        jnp.swapaxes(fast_down, 1, 2),
+        ttt_gain,
+        attn_gain,
         out_proj,
     )
 

time: 70.3 us -> 70.9 us (level)
  the two profiles are of different devices: /device:TPU:27 before, /device:TPU:25 now
where the time goes in v1:
time: 70.9 us; the launch traced here: 70.7 us
  Pallas kernels  69.1 us (97%)
  local copies, waits for them, and re-layouts  1.62 us (2%)
    pallas_call x1, Pallas kernels, local(): pl.pallas_call(functools.partial(kernel, n_seq, n_head), out_shape=jax.Sh...  69.1 us
    unnamed x1, local copies, waits for them, and re-layouts  1.62 us

profile of v1, /device:TPU:25, one launch (start us, length us, event | category | flops | bytes accessed | tf_op | source)
XLA Modules:
  0.0 70.7 jit_solution(10379557642016875957)
XLA Ops:
  0.0 69.1 %shard_map.118 = bf16[128,768]{1,0:T(8,128)(2,1)} custom-call(bf16[256,384]{1,0:T(8,128)(2,1)} %q_hbm.1, bf16[256,384]{1,0:T(8,128)(2,1)} %k_hbm.1, bf16[256,384]{1,0:T(8,128)(2,1)} %v_hbm.1, f32[2,256]{1,0:T(2,128)} %bitcast.4, f32[1,2]{1,0:T(1,128)} %decay_ref.1, f32[1,2]{1,0:T(1,128)} %bitcast.5, f32[2,192,384]{2,1,0:T(8,128)} %gate_hbm.1, ...), custom_call_target="tpu_custom_call" | custom-call | tf_op jit(solution)/shard_map/pallas_call | solution.py:525
  69.1 1.6 %copy.14 = bf16[128,768]{1,0:T(8,128)(2,1)} copy(bf16[128,768]{1,0:T(8,128)(2,1)} %shard_map.118) | data formatting | bytes 393216

commit v2 on v1

--- a/solution.py
+++ b/solution.py
@@ -84,6 +84,8 @@
     acc,
     top,
     total,
+    share_attn,
+    query_pair,
     mixed,
     p_out,
     p_in,
@@ -220,7 +222,62 @@
     for load in loads[2:5]:
         load.wait()
 
-    for h in range(heads):
+    mine_at = pl.multiple_of(core * part, part)
+    other_at = pl.multiple_of((1 - core) * part, part)
+
+    def pair_copy(source, target, send, recv, j, seq_pos):
+        return pltpu.make_async_remote_copy(
+            src_ref=source.at[j],
+            dst_ref=target.at[j],
+            send_sem=send.at[j],
+            recv_sem=recv.at[j],
+            device_id=(seq_pos, head),
+            device_id_type=MESH,
+        )
+
+    x_copy = lambda p: pair_copy(x_out, x_in, x_send, x_recv, p, sibling)
+    t_copy = lambda p: pair_copy(t_out, t_in, t_send, t_recv, p, across)
+    s_copy = lambda p: pair_copy(s_out, s_in, s_send, s_recv, p, onward)
+    h_copy = lambda p: pair_copy(h_out, h_in, h_send, h_recv, p, sibling)
+
+    def rows_at(p, base):
+        return pl.ds(pl.multiple_of(base + (p % SPLIT) * chunk, chunk), chunk)
+
+    @pl.when(group == 0)
+    def _():
+        s_in[...] = jnp.zeros(s_in.shape, BF)
+
+    first = core == 0
+
+    def of_pair(p):
+        j = p // SPLIT
+        h = j // 3
+        d_own = dec_own[pl.ds(h, 1), :][:, 0:1]
+        d_sib = dec_sib[pl.ds(h, 1), :][:, 0:1]
+        u_own = upd[j, rows_at(p, mine_at), :]
+        u_sib = x_in[p].astype(F32)
+        return (
+            jnp.where(first, d_own, d_sib),
+            jnp.where(first, d_sib, d_own),
+            jnp.where(first, u_own, u_sib),
+            jnp.where(first, u_sib, u_own),
+        )
+
+    def sum_pair(p, carry):
+        x_copy(p).wait_recv()
+        _, decay1, u0, u1 = of_pair(p)
+        both = decay1 * u0 + u1
+        t_own[p] = both
+        t_out[p] = both.astype(BF)
+        t_copy(p).start()
+        return carry
+
+    per_head = 3 * SPLIT
+
+    def sum_pairs(h):
+        lax.fori_loop(h * per_head, (h + 1) * per_head, sum_pair, 0)
+
+    def gradients(h):
         cols = slice(h * dim, (h + 1) * dim)
         key_norm = rms_rows(kv[own, 0].astype(F32)[:, cols])
         rate = jnp.broadcast_to(rates_ref[h : h + 1, :], (8, rows)).T[:, 0:1]
@@ -241,100 +298,49 @@
             size = jnp.sum(jnp.sum(grad * grad, axis=1, keepdims=True), axis=0, keepdims=True)
             upd[3 * h + i] = grad / (jnp.sqrt(size) + 1e-07)
 
-    def sweep(turn, carry):
-        for j in range(3 * heads):
-            current = upd[j]
-            low = current.astype(BF)
-            gram = dot1(low, low, NT)
-            gram_low = gram.astype(BF)
-            poly = coef_b * gram + coef_c * dot1(gram_low, gram_low)
-            upd[j] = coef_a * current + dot1(poly.astype(BF), low)
-
-        @pl.when(turn == 1)
-        def _():
+    def orthogonalize(h):
+        def sweep(turn, carry):
+            for j in range(3 * h, 3 * h + 3):
+                current = upd[j]
+                low = current.astype(BF)
+                gram = dot1(low, low, NT)
+                gram_low = gram.astype(BF)
+                poly = coef_b * gram + coef_c * dot1(gram_low, gram_low)
+                upd[j] = coef_a * current + dot1(poly.astype(BF), low)
+            return carry
+
+        lax.fori_loop(0, NS_STEPS, sweep, 0)
+        for p in range(h * per_head, (h + 1) * per_head):
+            j = p // SPLIT
+            if p % SPLIT == 0:
+                upd[j] = -step_ref[0:1, h : h + 1] * upd[j]
+            x_out[p] = upd[j, rows_at(p, other_at), :].astype(BF)
+            x_copy(p).start()
+
+    for h in range(heads):
+        gradients(h)
+        if h == 1:
             arrive(4, (3, 4, 5))
-
-        @pl.when(turn == 3)
-        def _():
-            arrive(2, (8,))
-
-        return carry
-
-    lax.fori_loop(0, NS_STEPS, sweep, 0)
-
-    mine_at = pl.multiple_of(core * part, part)
-    other_at = pl.multiple_of((1 - core) * part, part)
-
-    def pair_copy(source, target, send, recv, j, seq_pos):
-        return pltpu.make_async_remote_copy(
-            src_ref=source.at[j],
-            dst_ref=target.at[j],
-            send_sem=send.at[j],
-            recv_sem=recv.at[j],
-            device_id=(seq_pos, head),
-            device_id_type=MESH,
-        )
-
-    x_copy = lambda p: pair_copy(x_out, x_in, x_send, x_recv, p, sibling)
-    t_copy = lambda p: pair_copy(t_out, t_in, t_send, t_recv, p, across)
-    s_copy = lambda p: pair_copy(s_out, s_in, s_send, s_recv, p, onward)
-    h_copy = lambda p: pair_copy(h_out, h_in, h_send, h_recv, p, sibling)
-
-    def rows_at(p, base):
-        return pl.ds(pl.multiple_of(base + (p % SPLIT) * chunk, chunk), chunk)
-
-    for p in range(pieces):
-        j = p // SPLIT
-        if p % SPLIT == 0:
-            upd[j] = -step_ref[0:1, j // 3 : j // 3 + 1] * upd[j]
-        x_out[p] = upd[j, rows_at(p, other_at), :].astype(BF)
-        x_copy(p).start()
-    dec_copy.wait()
-    dec_chip[...] = dec_own[...] * dec_sib[...]
-    dec_chip_copy = pltpu.make_async_remote_copy(
-        src_ref=dec_chip,
-        dst_ref=dec_across,
-        send_sem=dec_sems.at[2],
-        recv_sem=dec_sems.at[3],
-        device_id=(across, head),
-        device_id_type=MESH,
-    )
-    dec_chip_copy.start()
-
-    @pl.when(group == 0)
-    def _():
-        s_in[...] = jnp.zeros(s_in.shape, BF)
-
-    first = core == 0
-
-    def of_pair(p):
-        j = p // SPLIT
-        h = j // 3
-        d_own = dec_own[pl.ds(h, 1), :][:, 0:1]
-        d_sib = dec_sib[pl.ds(h, 1), :][:, 0:1]
-        u_own = upd[j, rows_at(p, mine_at), :]
-        u_sib = x_in[p].astype(F32)
-        return (
-            jnp.where(first, d_own, d_sib),
-            jnp.where(first, d_sib, d_own),
-            jnp.where(first, u_own, u_sib),
-            jnp.where(first, u_sib, u_own),
-        )
-
-    def sum_pair(p, carry):
-        x_copy(p).wait_recv()
-        _, decay1, u0, u1 = of_pair(p)
-        both = decay1 * u0 + u1
-        t_own[p] = both
-        t_out[p] = both.astype(BF)
-        t_copy(p).start()
-        return carry
-
-    lax.fori_loop(0, pieces, sum_pair, 0)
+            pl.when(side == 1)(lambda: arrive(2, (8,)))
+        if h == 0:
+            dec_copy.wait()
+            dec_chip[...] = dec_own[...] * dec_sib[...]
+            dec_chip_copy = pltpu.make_async_remote_copy(
+                src_ref=dec_chip,
+                dst_ref=dec_across,
+                send_sem=dec_sems.at[2],
+                recv_sem=dec_sems.at[3],
+                device_id=(across, head),
+                device_id_type=MESH,
+            )
+            dec_chip_copy.start()
+        else:
+            sum_pairs(h - 1)
+        orthogonalize(h)
+    pl.when(side == 0)(lambda: arrive(2, (8,)))
+    arrive(8, (6, 7))
+    sum_pairs(heads - 1)
     dec_chip_copy.wait()
-
-    arrive(8, (6, 7))
-    arrive(6, (9,))
 
     near = side == 0
 
@@ -388,41 +394,49 @@
         jnp.int32, (rows, rows), 1
     )
 
-    def attend(distance, carry):
-        @pl.when(3 * group == distance)
-        def _():
-            chain()
-
-        @pl.when(me >= distance)
-        def _():
-            @pl.when(distance % 2 == 1)
-            def _():
-                await_block(distance)
-
-            slot = slot_of(distance)
-            back = gap + distance * rows
-            allowed = (back >= 0) & (back < WINDOW)
-            for h in range(heads):
-                cols = slice(starts[h], starts[h] + 256)
-                scores = dot1(qpad[h], kv[slot, 0, :, cols], NT) * scale
-                scores = jnp.where(allowed, scores, FAR)
-                old_top = top[h][:, 0:1]
-                new_top = jnp.maximum(old_top, jnp.max(scores, axis=1, keepdims=True))
-                weights = jnp.exp(scores - new_top)
-                shrink = jnp.exp(old_top - new_top)
-                total[h] = jnp.broadcast_to(
-                    total[h][:, 0:1] * shrink + jnp.sum(weights, axis=1, keepdims=True), (rows, 128)
-                )
-                acc[h] = acc[h] * shrink + dot1(weights.astype(BF), kv[slot, 1, :, cols])
-                top[h] = jnp.broadcast_to(new_top, (rows, 128))
-
-        return carry
-
-    lax.fori_loop(0, reach + 1, attend, 0)
-
-    @pl.when(3 * group > reach)
-    def _():
-        chain()
+    def attend(distance):
+        slot = slot_of(distance)
+        back = gap + distance * rows
+        for h in range(heads):
+            cols = slice(starts[h], starts[h] + 256)
+            scores = dot1(qpad[h], kv[slot, 0, :, cols], NT) * scale
+            if distance == 0:
+                scores = jnp.where(back >= 0, scores, FAR)
+            if distance == reach:
+                scores = jnp.where(back < WINDOW, scores, FAR)
+            old_top = top[h][:, 0:1]
+            new_top = jnp.maximum(old_top, jnp.max(scores, axis=1, keepdims=True))
+            weights = jnp.exp(scores - new_top)
+            shrink = jnp.exp(old_top - new_top)
+            total[h] = jnp.broadcast_to(
+                total[h][:, 0:1] * shrink + jnp.sum(weights, axis=1, keepdims=True), (rows, 128)
+            )
+            acc[h] = acc[h] * shrink + dot1(weights.astype(BF), kv[slot, 1, :, cols])
+            top[h] = jnp.broadcast_to(new_top, (rows, 128))
+
+    def turn_of(distance):
+        if distance % 2 == 1:
+            await_block(distance)
+        attend(distance)
+
+    early = []
+    for position, distance in enumerate((0, 1, 3, 2, 4, 8, 7, 5, 6)):
+        if position % 2 == 0 and position // 2 + 1 < n_group:
+            early.append(position // 2)
+            pl.when(group == position // 2)(chain)
+        if position == 6:
+            arrive(6, (9,))
+        pl.when(me >= distance)(functools.partial(turn_of, distance))
+
+    for h in range(heads):
+        cols = slice(h * dim, (h + 1) * dim)
+        begin = h * dim - starts[h]
+        attended = acc[h][:, begin : begin + dim] / total[h][:, 0:1]
+        share_attn[h] = rms_rows(attended) * again_ref[...].reshape(1, -1)[:, cols]
+        for i, piece in enumerate(halves(rms_rows(q_ref[...].astype(F32)[:, cols]))):
+            query_pair[h, i] = piece
+
+    pl.when(group > early[-1] if early else group >= 0)(chain)
 
     loads[6].wait()
     for p in range(pieces):
@@ -431,16 +445,13 @@
 
     for h in range(heads):
         cols = slice(h * dim, (h + 1) * dim)
-        query = halves(rms_rows(q_ref[...].astype(F32)[:, cols]))
+        query = (query_pair[h, 0], query_pair[h, 1])
         pre_gate = dot3(query, halves(gate_ref[h] + state[3 * h]))
         pre_up = dot3(query, halves(up_ref[h] + state[3 * h + 1]))
         hidden = pre_gate * jax.nn.sigmoid(pre_gate) * pre_up
         applied = dot3(halves(hidden), halves(downt[h] + state[3 * h + 2]), NT)
-        begin = h * dim - starts[h]
-        attended = acc[h][:, begin : begin + dim] / total[h][:, 0:1]
         mixed[h] = (
-            rms_rows(applied) * tgain_ref[...].reshape(1, -1)[:, cols]
-            + rms_rows(attended) * again_ref[...].reshape(1, -1)[:, cols]
+            rms_rows(applied) * tgain_ref[...].reshape(1, -1)[:, cols] + share_attn[h]
         ).astype(BF)
 
     share = rows // n_head
@@ -553,6 +564,8 @@
             pltpu.VMEM((heads, rows, 256), F32),
             pltpu.VMEM((heads, rows, 128), F32),
             pltpu.VMEM((heads, rows, 128), F32),
+            pltpu.VMEM((heads, rows, dim), F32),
+            pltpu.VMEM((heads, 2, rows, dim), BF),
             pltpu.VMEM((heads, rows, dim), BF),
             pltpu.VMEM((n_head - 1, share, width), BF),
             pltpu.VMEM((n_head - 1, share, width), BF),

time: 70.9 us -> 59.7 us (0.84)
  the two profiles are of different devices: /device:TPU:25 before, /device:TPU:17 now
where the time goes in v2:
time: 59.7 us; the launch traced here: 59.5 us
  Pallas kernels  57.9 us (97%)
  local copies, waits for them, and re-layouts  1.62 us (3%)
    pallas_call x1, Pallas kernels, local(): pl.pallas_call(functools.partial(kernel, n_seq, n_head), out_shape=jax.Sh...  57.9 us
    unnamed x1, local copies, waits for them, and re-layouts  1.62 us

profile of v2, /device:TPU:17, one launch (start us, length us, event | category | flops | bytes accessed | tf_op | source)
XLA Modules:
  0.0 59.5 jit_solution(12944500722380246083)
XLA Ops:
  0.0 57.9 %shard_map.118 = bf16[128,768]{1,0:T(8,128)(2,1)} custom-call(bf16[256,384]{1,0:T(8,128)(2,1)} %q_hbm.1, bf16[256,384]{1,0:T(8,128)(2,1)} %k_hbm.1, bf16[256,384]{1,0:T(8,128)(2,1)} %v_hbm.1, f32[2,256]{1,0:T(2,128)} %bitcast.4, f32[1,2]{1,0:T(1,128)} %decay_ref.1, f32[1,2]{1,0:T(1,128)} %bitcast.5, f32[2,192,384]{2,1,0:T(8,128)} %gate_hbm.1, ...), custom_call_target="tpu_custom_call" | custom-call | tf_op jit(solution)/shard_map/pallas_call | solution.py:536
  57.9 1.6 %copy.14 = bf16[128,768]{1,0:T(8,128)(2,1)} copy(bf16[128,768]{1,0:T(8,128)(2,1)} %shard_map.118) | data formatting | bytes 393216

commit v3 on v2

--- a/solution.py
+++ b/solution.py
@@ -39,8 +39,16 @@
     )
 
 
+def dot2(left, right):
+    return dot1(left, right[0]) + dot1(left, right[1])
+
+
+def rms_inverse(values):
+    return lax.rsqrt(jnp.mean(values * values, axis=-1, keepdims=True) + 1e-06)
+
+
 def rms_rows(values):
-    return values * lax.rsqrt(jnp.mean(values * values, axis=-1, keepdims=True) + 1e-06)
+    return values * rms_inverse(values)
 
 
 def kernel(
@@ -85,7 +93,8 @@
     top,
     total,
     share_attn,
-    query_pair,
+    query_low,
+    query_scale,
     mixed,
     p_out,
     p_in,
@@ -183,7 +192,7 @@
         (has_next & (me >= 4), slot_of(4), slot_of(8), 3, onward),
         (me >= 4, slot_of(4), slot_of(4), 4, across),
         (me >= 4, slot_of(4), slot_of(4), 5, sibling),
-        ((me >= 8) & (side == 1), slot_of(8), slot_of(8), 6, across),
+        (has_next & (me >= 4) & (side == 0), slot_of(2), slot_of(6), 6, onward),
         ((me >= 8) & (core == 1), slot_of(8), slot_of(8), 7, sibling),
         (me >= 2, slot_of(2), slot_of(2), 8, sibling),
         (me >= 6, slot_of(6), slot_of(6), 9, sibling),
@@ -279,20 +288,21 @@
 
     def gradients(h):
         cols = slice(h * dim, (h + 1) * dim)
-        key_norm = rms_rows(kv[own, 0].astype(F32)[:, cols])
-        rate = jnp.broadcast_to(rates_ref[h : h + 1, :], (8, rows)).T[:, 0:1]
-        err = -rate * kv[own, 1].astype(F32)[:, cols]
-        key_pair = halves(key_norm)
-        pre_gate = dot3(key_pair, halves(gate_ref[h]))
-        pre_up = dot3(key_pair, halves(up_ref[h]))
+        key = kv[own, 0].astype(F32)[:, cols]
+        value = kv[own, 1].astype(F32)[:, cols]
+        key_scale = rms_inverse(key)
+        rate = -jnp.broadcast_to(rates_ref[h : h + 1, :], (8, rows)).T[:, 0:1]
+        key_low = key.astype(BF)
+        pre_gate = key_scale * dot2(key_low, halves(gate_ref[h]))
+        pre_up = key_scale * dot2(key_low, halves(up_ref[h]))
         sig = jax.nn.sigmoid(pre_gate)
         active = pre_gate * sig
-        back = dot3(halves(err), halves(downt[h]))
-        key_t = halves(key_norm.T)
+        back = (rate * key_scale) * dot2(value.astype(BF), halves(downt[h]))
+        key_t = key.T.astype(BF)
         grads = (
-            dot3(key_t, halves(back * pre_up * (sig * (1.0 + pre_gate * (1.0 - sig))))),
-            dot3(key_t, halves(back * active)),
-            dot3(halves(err.T), halves(active * pre_up)),
+            dot2(key_t, halves(back * pre_up * (sig * (1.0 + pre_gate * (1.0 - sig))))),
+            dot2(key_t, halves(back * active)),
+            dot2(value.T.astype(BF), halves(rate * active * pre_up)),
         )
         for i, grad in enumerate(grads):
             size = jnp.sum(jnp.sum(grad * grad, axis=1, keepdims=True), axis=0, keepdims=True)
@@ -320,7 +330,6 @@
     for h in range(heads):
         gradients(h)
         if h == 1:
-            arrive(4, (3, 4, 5))
             pl.when(side == 1)(lambda: arrive(2, (8,)))
         if h == 0:
             dec_copy.wait()
@@ -337,8 +346,10 @@
         else:
             sum_pairs(h - 1)
         orthogonalize(h)
-    pl.when(side == 0)(lambda: arrive(2, (8,)))
-    arrive(8, (6, 7))
+        if h == 0:
+            arrive(4, (3, 4, 5))
+    pl.when(side == 0)(lambda: arrive(2, (6, 8)))
+    arrive(8, (7,))
     sum_pairs(heads - 1)
     dec_chip_copy.wait()
 
@@ -433,8 +444,9 @@
         begin = h * dim - starts[h]
         attended = acc[h][:, begin : begin + dim] / total[h][:, 0:1]
         share_attn[h] = rms_rows(attended) * again_ref[...].reshape(1, -1)[:, cols]
-        for i, piece in enumerate(halves(rms_rows(q_ref[...].astype(F32)[:, cols]))):
-            query_pair[h, i] = piece
+        query = q_ref[...].astype(F32)[:, cols]
+        query_low[h] = query.astype(BF)
+        query_scale[h] = jnp.broadcast_to(rms_inverse(query), (rows, 128))
 
     pl.when(group > early[-1] if early else group >= 0)(chain)
 
@@ -445,9 +457,10 @@
 
     for h in range(heads):
         cols = slice(h * dim, (h + 1) * dim)
-        query = (query_pair[h, 0], query_pair[h, 1])
-        pre_gate = dot3(query, halves(gate_ref[h] + state[3 * h]))
-        pre_up = dot3(query, halves(up_ref[h] + state[3 * h + 1]))
+        query = query_low[h]
+        scale_q = query_scale[h][:, 0:1]
+        pre_gate = scale_q * dot2(query, halves(gate_ref[h] + state[3 * h]))
+        pre_up = scale_q * dot2(query, halves(up_ref[h] + state[3 * h + 1]))
         hidden = pre_gate * jax.nn.sigmoid(pre_gate) * pre_up
         applied = dot3(halves(hidden), halves(downt[h] + state[3 * h + 2]), NT)
         mixed[h] = (
@@ -565,7 +578,8 @@
             pltpu.VMEM((heads, rows, 128), F32),
             pltpu.VMEM((heads, rows, 128), F32),
             pltpu.VMEM((heads, rows, dim), F32),
-            pltpu.VMEM((heads, 2, rows, dim), BF),
+            pltpu.VMEM((heads, rows, dim), BF),
+            pltpu.VMEM((heads, rows, 128), F32),
             pltpu.VMEM((heads, rows, dim), BF),
             pltpu.VMEM((n_head - 1, share, width), BF),
             pltpu.VMEM((n_head - 1, share, width), BF),

time: 59.7 us -> 57.2 us (0.958)
  Pallas kernels: 57.9 us -> 55.4 us
    pallas_call x1, Pallas kernels: 57.9 us -> 55.4 us  [local(): pl.pallas_call(functools.partial(kernel, n_seq, n_head), out_shape=jax.Sh...]
where the time goes in v3:
time: 57.2 us; the launch traced here: 57 us
  Pallas kernels  55.4 us (97%)
  local copies, waits for them, and re-layouts  1.62 us (3%)
    pallas_call x1, Pallas kernels, local(): pl.pallas_call(functools.partial(kernel, n_seq, n_head), out_shape=jax.Sh...  55.4 us
    unnamed x1, local copies, waits for them, and re-layouts  1.62 us

profile of v3, /device:TPU:17, one launch (start us, length us, event | category | flops | bytes accessed | tf_op | source)
XLA Modules:
  0.0 57.0 jit_solution(54561705028759810)
XLA Ops:
  0.0 55.4 %shard_map.118 = bf16[128,768]{1,0:T(8,128)(2,1)} custom-call(bf16[256,384]{1,0:T(8,128)(2,1)} %q_hbm.1, bf16[256,384]{1,0:T(8,128)(2,1)} %k_hbm.1, bf16[256,384]{1,0:T(8,128)(2,1)} %v_hbm.1, f32[2,256]{1,0:T(2,128)} %bitcast.4, f32[1,2]{1,0:T(1,128)} %decay_ref.1, f32[1,2]{1,0:T(1,128)} %bitcast.5, f32[2,192,384]{2,1,0:T(8,128)} %gate_hbm.1, ...), custom_call_target="tpu_custom_call" | custom-call | tf_op jit(solution)/shard_map/pallas_call | solution.py:549
  55.4 1.6 %copy.14 = bf16[128,768]{1,0:T(8,128)(2,1)} copy(bf16[128,768]{1,0:T(8,128)(2,1)} %shard_map.118) | data formatting | bytes 393216

commit v4 on v3

--- a/solution.py
+++ b/solution.py
@@ -327,6 +327,43 @@
             x_out[p] = upd[j, rows_at(p, other_at), :].astype(BF)
             x_copy(p).start()
 
+    near = side == 0
+
+    def chain(head_id):
+        def link(p, carry):
+            h = p // SPLIT // 3
+            t_copy(p).wait_recv()
+
+            @pl.when(group > 0)
+            def _():
+                s_copy(p).wait_recv()
+
+            c_own = dec_chip[pl.ds(h, 1), :][:, 0:1]
+            c_far = dec_across[pl.ds(h, 1), :][:, 0:1]
+            chip0 = jnp.where(near, c_own, c_far)
+            chip1 = jnp.where(near, c_far, c_own)
+            t_far = t_in[p].astype(F32)
+            t_mine = t_own[p]
+            t0 = jnp.where(near, t_mine, t_far)
+            t1 = jnp.where(near, t_far, t_mine)
+            enter = s_in[p].astype(F32)
+            halfway = chip0 * enter + t0
+
+            @pl.when(has_next)
+            def _():
+                s_out[p] = (chip1 * halfway + t1).astype(BF)
+                s_copy(p).start()
+
+            decay0, _, u0, _ = of_pair(p)
+            before = jnp.where(near, enter, halfway)
+            middle = decay0 * before + u0
+            h_out[p] = jnp.where(first, middle, before).astype(BF)
+            h_copy(p).start()
+            state[p // SPLIT, rows_at(p, mine_at), :] = jnp.where(first, before, middle)
+            return carry
+
+        lax.fori_loop(head_id * per_head, (head_id + 1) * per_head, link, 0)
+
     for h in range(heads):
         gradients(h)
         if h == 1:
@@ -344,51 +381,16 @@
             )
             dec_chip_copy.start()
         else:
+            if h == 1:
+                dec_chip_copy.wait()
             sum_pairs(h - 1)
         orthogonalize(h)
         if h == 0:
             arrive(4, (3, 4, 5))
+    pl.when(group == 0)(lambda: chain(0))
+    sum_pairs(heads - 1)
     pl.when(side == 0)(lambda: arrive(2, (6, 8)))
     arrive(8, (7,))
-    sum_pairs(heads - 1)
-    dec_chip_copy.wait()
-
-    near = side == 0
-
-    def chain():
-        def link(p, carry):
-            h = p // SPLIT // 3
-            t_copy(p).wait_recv()
-
-            @pl.when(group > 0)
-            def _():
-                s_copy(p).wait_recv()
-
-            c_own = dec_chip[pl.ds(h, 1), :][:, 0:1]
-            c_far = dec_across[pl.ds(h, 1), :][:, 0:1]
-            chip0 = jnp.where(near, c_own, c_far)
-            chip1 = jnp.where(near, c_far, c_own)
-            t_far = t_in[p].astype(F32)
-            t_mine = t_own[p]
-            t0 = jnp.where(near, t_mine, t_far)
-            t1 = jnp.where(near, t_far, t_mine)
-            enter = s_in[p].astype(F32)
-            halfway = chip0 * enter + t0
-
-            @pl.when(has_next)
-            def _():
-                s_out[p] = (chip1 * halfway + t1).astype(BF)
-                s_copy(p).start()
-
-            decay0, _, u0, _ = of_pair(p)
-            before = jnp.where(near, enter, halfway)
-            middle = decay0 * before + u0
-            h_out[p] = jnp.where(first, middle, before).astype(BF)
-            h_copy(p).start()
-            state[p // SPLIT, rows_at(p, mine_at), :] = jnp.where(first, before, middle)
-            return carry
-
-        lax.fori_loop(0, pieces, link, 0)
 
     loads[5].wait()
     lane = lax.broadcasted_iota(jnp.int32, (rows, 256), 1)
@@ -430,13 +432,20 @@
             await_block(distance)
         attend(distance)
 
-    early = []
+    last_at = {0: 2, 1: 6}
+
+    def rest():
+        for h in range(1, heads):
+            chain(h)
+
     for position, distance in enumerate((0, 1, 3, 2, 4, 8, 7, 5, 6)):
-        if position % 2 == 0 and position // 2 + 1 < n_group:
-            early.append(position // 2)
-            pl.when(group == position // 2)(chain)
         if position == 6:
             arrive(6, (9,))
+        if position in (2, 4, 6, 8) and position // 2 < n_group:
+            pl.when(group == position // 2)(lambda: chain(0))
+        for g, at in last_at.items():
+            if at == position:
+                pl.when(group == g)(rest)
         pl.when(me >= distance)(functools.partial(turn_of, distance))
 
     for h in range(heads):
@@ -448,14 +457,16 @@
         query_low[h] = query.astype(BF)
         query_scale[h] = jnp.broadcast_to(rms_inverse(query), (rows, 128))
 
-    pl.when(group > early[-1] if early else group >= 0)(chain)
-
+    pl.when(group > 4)(lambda: chain(0))
+
+    pl.when((group > 1) & has_next)(rest)
     loads[6].wait()
-    for p in range(pieces):
-        h_copy(p).wait_recv()
-        state[p // SPLIT, rows_at(p, other_at), :] = h_in[p].astype(F32)
-
     for h in range(heads):
+        if h == 1:
+            pl.when((group > 1) & (group + 1 == n_group))(rest)
+        for p in range(h * per_head, (h + 1) * per_head):
+            h_copy(p).wait_recv()
+            state[p // SPLIT, rows_at(p, other_at), :] = h_in[p].astype(F32)
         cols = slice(h * dim, (h + 1) * dim)
         query = query_low[h]
         scale_q = query_scale[h][:, 0:1]

time: 57.2 us -> 62.3 us (1.089)
  the two profiles are of different devices: /device:TPU:17 before, /device:TPU:25 now
where the time goes in v4:
time: 62.3 us; the launch traced here: 61.4 us
  Pallas kernels  59.8 us (96%)
  local copies, waits for them, and re-layouts  1.62 us (3%)
    pallas_call x1, Pallas kernels, local(): pl.pallas_call(functools.partial(kernel, n_seq, n_head), out_shape=jax.Sh...  59.8 us
    unnamed x1, local copies, waits for them, and re-layouts  1.62 us

profile of v4, /device:TPU:25, one launch (start us, length us, event | category | flops | bytes accessed | tf_op | source)
XLA Modules:
  0.0 61.4 jit_solution(12604314114101017818)
XLA Ops:
  0.0 59.8 %shard_map.118 = bf16[128,768]{1,0:T(8,128)(2,1)} custom-call(bf16[256,384]{1,0:T(8,128)(2,1)} %q_hbm.1, bf16[256,384]{1,0:T(8,128)(2,1)} %k_hbm.1, bf16[256,384]{1,0:T(8,128)(2,1)} %v_hbm.1, f32[2,256]{1,0:T(2,128)} %bitcast.4, f32[1,2]{1,0:T(1,128)} %decay_ref.1, f32[1,2]{1,0:T(1,128)} %bitcast.5, f32[2,192,384]{2,1,0:T(8,128)} %gate_hbm.1, ...), custom_call_target="tpu_custom_call" | custom-call | tf_op jit(solution)/shard_map/pallas_call | solution.py:560
  59.8 1.6 %copy.14 = bf16[128,768]{1,0:T(8,128)(2,1)} copy(bf16[128,768]{1,0:T(8,128)(2,1)} %shard_map.118) | data formatting | bytes 393216

commit v5 on v4

--- a/solution.py
+++ b/solution.py
@@ -108,6 +108,7 @@
     t_recv,
     s_send,
     s_recv,
+    y_send,
     h_send,
     h_recv,
     p_send,
@@ -247,6 +248,7 @@
     x_copy = lambda p: pair_copy(x_out, x_in, x_send, x_recv, p, sibling)
     t_copy = lambda p: pair_copy(t_out, t_in, t_send, t_recv, p, across)
     s_copy = lambda p: pair_copy(s_out, s_in, s_send, s_recv, p, onward)
+    y_copy = lambda p: pair_copy(s_in, s_in, y_send, s_recv, p, across)
     h_copy = lambda p: pair_copy(h_out, h_in, h_send, h_recv, p, sibling)
 
     def rows_at(p, base):
@@ -255,6 +257,10 @@
     @pl.when(group == 0)
     def _():
         s_in[...] = jnp.zeros(s_in.shape, BF)
+
+    @pl.when(side == 0)
+    def _():
+        t_in[...] = jnp.zeros(t_in.shape, BF)
 
     first = core == 0
 
@@ -277,8 +283,12 @@
         _, decay1, u0, u1 = of_pair(p)
         both = decay1 * u0 + u1
         t_own[p] = both
-        t_out[p] = both.astype(BF)
-        t_copy(p).start()
+
+        @pl.when(side == 0)
+        def _():
+            t_out[p] = both.astype(BF)
+            t_copy(p).start()
+
         return carry
 
     per_head = 3 * SPLIT
@@ -332,11 +342,17 @@
     def chain(head_id):
         def link(p, carry):
             h = p // SPLIT // 3
-            t_copy(p).wait_recv()
+            @pl.when(side == 1)
+            def _():
+                t_copy(p).wait_recv()
 
             @pl.when(group > 0)
             def _():
                 s_copy(p).wait_recv()
+
+            @pl.when((group > 0) & (side == 1))
+            def _():
+                y_copy(p).start()
 
             c_own = dec_chip[pl.ds(h, 1), :][:, 0:1]
             c_far = dec_across[pl.ds(h, 1), :][:, 0:1]
@@ -349,7 +365,7 @@
             enter = s_in[p].astype(F32)
             halfway = chip0 * enter + t0
 
-            @pl.when(has_next)
+            @pl.when(has_next & (side == 1))
             def _():
                 s_out[p] = (chip1 * halfway + t1).astype(BF)
                 s_copy(p).start()
@@ -387,7 +403,7 @@
         orthogonalize(h)
         if h == 0:
             arrive(4, (3, 4, 5))
-    pl.when(group == 0)(lambda: chain(0))
+    pl.when((group == 0) & (side == 1))(lambda: chain(0))
     sum_pairs(heads - 1)
     pl.when(side == 0)(lambda: arrive(2, (6, 8)))
     arrive(8, (7,))
@@ -442,10 +458,10 @@
         if position == 6:
             arrive(6, (9,))
         if position in (2, 4, 6, 8) and position // 2 < n_group:
-            pl.when(group == position // 2)(lambda: chain(0))
+            pl.when((group == position // 2) & (side == 1))(lambda: chain(0))
         for g, at in last_at.items():
             if at == position:
-                pl.when(group == g)(rest)
+                pl.when((group == g) & (side == 1))(rest)
         pl.when(me >= distance)(functools.partial(turn_of, distance))
 
     for h in range(heads):
@@ -457,13 +473,13 @@
         query_low[h] = query.astype(BF)
         query_scale[h] = jnp.broadcast_to(rms_inverse(query), (rows, 128))
 
-    pl.when(group > 4)(lambda: chain(0))
-
-    pl.when((group > 1) & has_next)(rest)
+    pl.when((group > 4) | (side == 0))(lambda: chain(0))
+
+    pl.when((group > 1) & has_next & (side == 1))(rest)
     loads[6].wait()
     for h in range(heads):
         if h == 1:
-            pl.when((group > 1) & (group + 1 == n_group))(rest)
+            pl.when((side == 0) | ((group > 1) & (group + 1 == n_group)))(rest)
         for p in range(h * per_head, (h + 1) * per_head):
             h_copy(p).wait_recv()
             state[p // SPLIT, rows_at(p, other_at), :] = h_in[p].astype(F32)
@@ -518,10 +534,17 @@
 
     for p in range(pieces):
         x_copy(p).wait_send()
-        t_copy(p).wait_send()
         h_copy(p).wait_send()
 
-        @pl.when(has_next)
+        @pl.when(side == 0)
+        def _():
+            t_copy(p).wait_send()
+
+        @pl.when((group > 0) & (side == 1))
+        def _():
+            y_copy(p).wait_send()
+
+        @pl.when(has_next & (side == 1))
         def _():
             s_copy(p).wait_send()
 
@@ -606,6 +629,7 @@
             dma((pieces,)),
             dma((pieces,)),
             dma((pieces,)),
+            dma((pieces,)),
             dma((n_head - 1,)),
             dma((n_head - 1,)),
         ],

time: 62.3 us -> 58.3 us (0.936)
  Pallas kernels: 59.8 us -> 56.1 us
    pallas_call x1, Pallas kernels: 59.8 us -> 56.1 us  [local(): pl.pallas_call(functools.partial(kernel, n_seq, n_head), out_shape=jax.Sh...]
where the time goes in v5:
time: 58.3 us; the launch traced here: 57.7 us
  Pallas kernels  56.1 us (96%)
  local copies, waits for them, and re-layouts  1.62 us (3%)
    pallas_call x1, Pallas kernels, local(): pl.pallas_call(functools.partial(kernel, n_seq, n_head), out_shape=jax.Sh...  56.1 us
    unnamed x1, local copies, waits for them, and re-layouts  1.62 us

profile of v5, /device:TPU:25, one launch (start us, length us, event | category | flops | bytes accessed | tf_op | source)
XLA Modules:
  0.0 57.7 jit_solution(9038473150340439703)
XLA Ops:
  0.0 56.1 %shard_map.118 = bf16[128,768]{1,0:T(8,128)(2,1)} custom-call(bf16[256,384]{1,0:T(8,128)(2,1)} %q_hbm.1, bf16[256,384]{1,0:T(8,128)(2,1)} %k_hbm.1, bf16[256,384]{1,0:T(8,128)(2,1)} %v_hbm.1, f32[2,256]{1,0:T(2,128)} %bitcast.4, f32[1,2]{1,0:T(1,128)} %decay_ref.1, f32[1,2]{1,0:T(1,128)} %bitcast.5, f32[2,192,384]{2,1,0:T(8,128)} %gate_hbm.1, ...), custom_call_target="tpu_custom_call" | custom-call | tf_op jit(solution)/shard_map/pallas_call | solution.py:583
  56.1 1.6 %copy.14 = bf16[128,768]{1,0:T(8,128)(2,1)} copy(bf16[128,768]{1,0:T(8,128)(2,1)} %shard_map.118) | data formatting | bytes 393216

commit v6 on v5

--- a/solution.py
+++ b/solution.py
@@ -448,7 +448,7 @@
             await_block(distance)
         attend(distance)
 
-    last_at = {0: 2, 1: 6}
+    last_at = {0: 2, 1: 4, 2: 6}
 
     def rest():
         for h in range(1, heads):
@@ -475,7 +475,7 @@
 
     pl.when((group > 4) | (side == 0))(lambda: chain(0))
 
-    pl.when((group > 1) & has_next & (side == 1))(rest)
+    pl.when((group > 2) & has_next & (side == 1))(rest)
     loads[6].wait()
     for h in range(heads):
         if h == 1:

time: 58.3 us -> 55.7 us (0.955)
  Pallas kernels: 56.1 us -> 53.9 us
    pallas_call x1, Pallas kernels: 56.1 us -> 53.9 us  [local(): pl.pallas_call(functools.partial(kernel, n_seq, n_head), out_shape=jax.Sh...]
where the time goes in v6:
time: 55.7 us; the launch traced here: 55.5 us
  Pallas kernels  53.9 us (97%)
  local copies, waits for them, and re-layouts  1.62 us (3%)
    pallas_call x1, Pallas kernels, local(): pl.pallas_call(functools.partial(kernel, n_seq, n_head), out_shape=jax.Sh...  53.9 us
    unnamed x1, local copies, waits for them, and re-layouts  1.62 us

profile of v6, /device:TPU:25, one launch (start us, length us, event | category | flops | bytes accessed | tf_op | source)
XLA Modules:
  0.0 55.5 jit_solution(7081480240881434830)
XLA Ops:
  0.0 53.9 %shard_map.118 = bf16[128,768]{1,0:T(8,128)(2,1)} custom-call(bf16[256,384]{1,0:T(8,128)(2,1)} %q_hbm.1, bf16[256,384]{1,0:T(8,128)(2,1)} %k_hbm.1, bf16[256,384]{1,0:T(8,128)(2,1)} %v_hbm.1, f32[2,256]{1,0:T(2,128)} %bitcast.4, f32[1,2]{1,0:T(1,128)} %decay_ref.1, f32[1,2]{1,0:T(1,128)} %bitcast.5, f32[2,192,384]{2,1,0:T(8,128)} %gate_hbm.1, ...), custom_call_target="tpu_custom_call" | custom-call | tf_op jit(solution)/shard_map/pallas_call | solution.py:583
  53.9 1.6 %copy.14 = bf16[128,768]{1,0:T(8,128)(2,1)} copy(bf16[128,768]{1,0:T(8,128)(2,1)} %shard_map.118) | data formatting | bytes 393216
